TPU v7x, 128 devices: a whole 4x4x4 slice. The times are simulated.
128 devices in a mesh: grp: 4 (over x_lo, core), scan: 32 (over z, y, x_hi).
Axes of the slice: x: 4 (x_hi: 2, x_lo: 2; x = x_hi * 2 + x_lo), y: 4, z: 4, core: 2. Of those that a mesh axis runs over, the one named last changes fastest.
Arguments:
- projection: float32 [8, 2, 256, 4096], P('grp', None, None, 'scan'), may hold values from -6 to 6
- illumination: float32 [2, 256, 256], replicated, may hold values from -6 to 6
- amplitude: float32 [8, 128, 256, 256], P('grp', 'scan'), may hold values from 0 to 2
- offsets: int32 [8, 128], P('grp', 'scan'), may hold values from -128 to 3968, as said below
Outputs:
- gradient: float32 [8, 2, 256, 4096], P(None, None, ('grp', 'scan'))
Inputs may be any that keep to these rules, and one draw needn't show every extreme that they name: `offsets`: for every angle, scan position j has an offset between (j // 4) * 128 - 256 // 2 and that value plus 128; in each aligned block of 4 positions the first takes the lower end and the second the upper end.
All inputs are finite; a program needn't handle non-finite values.
Results may differ from a plain program's by a relative error of at most 0.0003.
Values sent between devices are 32-bit elements; how exact they have to be, the bound alone decides.
A program may use at most 64 MiB of HBM per device.

v0:
```python
import math

import jax
import jax.numpy as jnp
from jax import lax
from jax.sharding import PartitionSpec as P

highest = lax.Precision.HIGHEST


def passed_along(value, axis, steps):
    count = lax.axis_size(axis)
    first, last = (max(0, -steps), min(count, count - steps))
    return lax.ppermute(value, axis, [(source, source + steps) for source in range(first, last)])


def dft_tables(points):
    index = jnp.arange(points, dtype=jnp.int32)
    phase = (index[:, None] * index[None, :] % points).astype(jnp.float32) * (
        2.0 * math.pi / points
    )
    norm_scale = 1.0 / math.sqrt(points)
    return (jnp.cos(phase) * norm_scale, -jnp.sin(phase) * norm_scale)


def combine_parts(first_term, second_term):
    return jnp.stack(
        [first_term[:, 0] - second_term[:, 1], first_term[:, 1] + second_term[:, 0]], axis=1
    )


def transform(table_real, table_imag, field):
    first_term = jnp.einsum("ij,ncjk->ncik", table_real, field, precision=highest)
    second_term = jnp.einsum("ij,ncjk->ncik", table_imag, field, precision=highest)
    middle = combine_parts(first_term, second_term)
    first_term = jnp.einsum("ncjk,kl->ncjl", middle, table_real, precision=highest)
    second_term = jnp.einsum("ncjk,kl->ncjl", middle, table_imag, precision=highest)
    return combine_parts(first_term, second_term)


def patch_gradients(windows, amplitude, illumination, table_real, table_imag):
    illum_real = illumination[0][None]
    illum_imag = illumination[1][None]
    wave_real = illum_real * windows[:, 0] - illum_imag * windows[:, 1]
    wave_imag = illum_real * windows[:, 1] + illum_imag * windows[:, 0]
    far_field = transform(table_real, table_imag, jnp.stack([wave_real, wave_imag], axis=1))
    magnitude = jnp.sqrt(far_field[:, 0] * far_field[:, 0] + far_field[:, 1] * far_field[:, 1])
    factor = 1.0 - amplitude / jnp.maximum(magnitude, 0.5)
    residual_field = far_field * factor[:, None]
    back_field = transform(table_real, -table_imag, residual_field)
    grad_real = illum_real * back_field[:, 0] + illum_imag * back_field[:, 1]
    grad_imag = illum_real * back_field[:, 1] - illum_imag * back_field[:, 0]
    return jnp.stack([grad_real, grad_imag], axis=1)


def cut_windows(column_strip, starts, width):

    def one_angle(strip_angle, angle_starts):
        return jax.vmap(
            lambda start_col: lax.dynamic_slice_in_dim(strip_angle, start_col, width, 2)
        )(angle_starts)

    return jax.vmap(one_angle)(column_strip, starts)


def accumulate(patch_grad, starts, strip_width):
    slot_count = starts.shape[1]
    width = patch_grad.shape[-1]
    initial = jnp.zeros((patch_grad.shape[0], 2, patch_grad.shape[3], strip_width), jnp.float32)

    def add_patch(angle_sum, piece, start_col):
        current = lax.dynamic_slice_in_dim(angle_sum, start_col, width, 2)
        return lax.dynamic_update_slice_in_dim(angle_sum, current + piece, start_col, 2)

    def loop_step(slot, summed):
        pieces = lax.dynamic_index_in_dim(patch_grad, slot, 1, keepdims=False)
        columns = lax.dynamic_index_in_dim(starts, slot, 1, keepdims=False)
        return jax.vmap(add_patch)(summed, pieces, columns)

    return lax.fori_loop(0, slot_count, loop_step, initial)


def per_device(projection, illumination, amplitude, offsets):
    angle_count, _, row_count, tile_cols = projection.shape
    patch_width = illumination.shape[1]
    slot_count = offsets.shape[1]
    reach_tiles = patch_width // (2 * tile_cols)
    table_real, table_imag = dft_tables(patch_width)
    pieces = []
    for shift_step in range(-reach_tiles, reach_tiles + 1):
        if shift_step == 0:
            pieces.append(projection)
        else:
            pieces.append(passed_along(projection, "scan", -shift_step))
    column_strip = jnp.concatenate(pieces, axis=3)
    starts = offsets - (lax.axis_index("scan") * tile_cols - reach_tiles * tile_cols)
    windows = cut_windows(column_strip, starts, patch_width)
    patch_grad = patch_gradients(
        windows.reshape(angle_count * slot_count, 2, row_count, patch_width),
        amplitude.reshape(angle_count * slot_count, row_count, patch_width),
        illumination,
        table_real,
        table_imag,
    )
    patch_grad = patch_grad.reshape(angle_count, slot_count, 2, row_count, patch_width)
    summed = accumulate(patch_grad, starts, column_strip.shape[3])
    tile_sum = lax.slice_in_dim(
        summed, reach_tiles * tile_cols, (reach_tiles + 1) * tile_cols, axis=3
    )
    for segment in range(2 * reach_tiles + 1):
        if segment != reach_tiles:
            part_cols = lax.slice_in_dim(
                summed, segment * tile_cols, (segment + 1) * tile_cols, axis=3
            )
            tile_sum = tile_sum + passed_along(part_cols, "scan", segment - reach_tiles)
    group_count = lax.axis_size("grp")
    scan_count = lax.axis_size("scan")
    received = lax.all_to_all(
        tile_sum[None], ("grp", "scan"), split_axis=3, concat_axis=0, tiled=True
    )
    slice_rows = received.shape[3]
    received = received.reshape(group_count, scan_count, angle_count, 2, slice_rows, tile_cols)
    received = jnp.transpose(received, (0, 2, 3, 4, 1, 5))
    gradient = received.reshape(group_count * angle_count, 2, slice_rows, scan_count * tile_cols)
    return gradient


def solution(mesh):
    placed = (P("grp", None, None, "scan"), P(), P("grp", "scan", None, None), P("grp", "scan"))
    return jax.shard_map(
        per_device,
        mesh=mesh,
        in_specs=placed,
        out_specs=P(None, None, ("grp", "scan"), None),
        check_vma=False,
    )
```

profile of v0, /device:TPU:1, one launch (start us, length us, event | category | flops | bytes accessed | tf_op | source)
XLA Modules:
  0.0 293.4 jit_solution(12048634060215615626)
XLA Ops:
  1.3 5.5 %collective-permute-start = (f32[2,2,256,128]{2,1,0,3:T(2,128)S(1)}, f32[2,2,256,128]{2,1,0,3:T(2,128)S(1)}, u32[]{:S(2)}, u32[]{:S(2)}) collective-permute-start(f32[2,2,256,128]{2,1,0,3:T(2,128)S(1)} %copy.74), channel_id=1, source_target_pairs={{0,1},{1,2},{2,3},{3,4},{4,5},{5,6},{6,7},{7,8},{8,9},{9,10},{10,1... | collective-permute-start | bytes 1572872 | tf_op jit(solution)/shard_map/ppermute | solution.py:14
  10.2 7.1 %collective-permute-done = f32[2,2,256,128]{2,1,0,3:T(2,128)S(1)} collective-permute-done((f32[2,2,256,128]{2,1,0,3:T(2,128)S(1)}, f32[2,2,256,128]{2,1,0,3:T(2,128)S(1)}, u32[]{:S(2)}, u32[]{:S(2)}) %collective-permute-start) | collective-permute-done | bytes 524320 | tf_op jit(solution)/shard_map/ppermute | solution.py:14
  17.4 13.3 %collective-permute-done.1 = f32[2,2,256,128]{2,1,0,3:T(2,128)} collective-permute-done((f32[2,2,256,128]{2,1,0,3:T(2,128)S(1)}, f32[2,2,256,128]{2,1,0,3:T(2,128)}, u32[]{:S(2)}, u32[]{:S(2)}) %collective-permute-start.1) | collective-permute-done | bytes 524320 | tf_op jit(solution)/shard_map/ppermute | solution.py:14
  32.4 6.9 %gather_fusion.1 = f32[8,2,256,256]{2,1,3,0:T(2,128)} fusion(f32[2,2,256,384]{2,1,0,3:T(2,128)S(1)} %pad_maximum_fusion.14, s32[8]{0:T(128)S(1)} %reshape.62), kind=kCustom, calls=%fused_computation.1 | custom fusion | bytes 8388736 | tf_op jit(solution)/shard_map/vmap(vmap())/gather | solution.py:60
  39.3 7.5 %fusion.93 = (f32[8,1,256,256]{2,1,3,0:T(1,128)S(1)}, f32[8,1,256,256]{2,1,3,0:T(1,128)S(1)}) fusion(f32[8,2,256,256]{2,1,3,0:T(2,128)} %gather_fusion.1), kind=kLoop, calls=%fused_computation.129 | loop fusion | bytes 8388608 | tf_op jit(solution)/shard_map/slice | solution.py:44
  47.6 4.6 %fusion.10 = f32[8,2,256,256]{2,3,1,0:T(8,128)S(1)} fusion(f32[8,1,256,256]{2,3,1,0:T(8,128)S(1)} %get-tuple-element.143, f32[8,1,256,256]{2,3,1,0:T(8,128)S(1)} %get-tuple-element.142), kind=kOutput, calls=%fused_computation.26 | convolution fusion | flops 3223257088 | bytes 8388608 | tf_op jit(solution)/shard_map/ij,ncjk->ncik/dot_general | solution.py:33
  52.2 4.8 %fusion.11 = f32[8,2,256,256]{2,3,1,0:T(8,128)S(1)} fusion(f32[8,1,256,256]{2,3,1,0:T(8,128)S(1)} %get-tuple-element.143, f32[8,1,256,256]{2,3,1,0:T(8,128)S(1)} %get-tuple-element.142), kind=kOutput, calls=%fused_computation.27 | convolution fusion | flops 3223322624 | bytes 8388608 | tf_op jit(solution)/shard_map/ij,ncjk->ncik/dot_general | solution.py:34
  57.7 8.3 %fusion.3 = f32[8,2,256,256]{3,2,1,0:T(8,128)S(1)} fusion(f32[8,1,256,256]{2,3,1,0:T(8,128)S(1)} %get-tuple-element.141, f32[8,1,256,256]{2,3,1,0:T(8,128)S(1)} %get-tuple-element.140), kind=kOutput, calls=%fused_computation.19 | convolution fusion | flops 3223257088 | bytes 8388608 | tf_op jit(solution)/shard_map/ncjk,kl->ncjl/dot_general | solution.py:36
  66.0 8.7 %fusion.2 = f32[8,2,256,256]{3,2,1,0:T(8,128)S(1)} fusion(f32[8,1,256,256]{2,3,1,0:T(8,128)S(1)} %get-tuple-element.141, f32[8,1,256,256]{2,3,1,0:T(8,128)S(1)} %get-tuple-element.140), kind=kOutput, calls=%fused_computation.18 | convolution fusion | flops 3223322624 | bytes 8388608 | tf_op jit(solution)/shard_map/ncjk,kl->ncjl/dot_general | solution.py:37
  75.9 8.2 %fusion.8 = f32[8,2,256,256]{2,3,1,0:T(8,128)S(1)} fusion(f32[8,1,256,256]{3,2,1,0:T(8,128)S(1)} %get-tuple-element.129, f32[8,1,256,256]{3,2,1,0:T(8,128)S(1)} %get-tuple-element.128, f32[8,256,256]{2,1,0:T(8,128)S(1)} %get-tuple-element.127), kind=kOutput, calls=%fused_computation.24 | convolution fusion | flops 3224305664 | bytes 10485760 | tf_op jit(solution)/shard_map/ij,ncjk->ncik/dot_general | solution.py:33
  84.0 8.0 %fusion.9 = f32[8,2,256,256]{2,3,1,0:T(8,128)S(1)} fusion(f32[8,1,256,256]{3,2,1,0:T(8,128)S(1)} %get-tuple-element.129, f32[8,1,256,256]{3,2,1,0:T(8,128)S(1)} %get-tuple-element.128, f32[8,256,256]{2,1,0:T(8,128)S(1)} %get-tuple-element.127), kind=kOutput, calls=%fused_computation.25 | convolution fusion | flops 3224436736 | bytes 10485760 | tf_op jit(solution)/shard_map/ij,ncjk->ncik/dot_general | solution.py:34
  92.6 5.7 %fusion.1 = f32[8,2,256,256]{2,3,1,0:T(8,128)S(1)} fusion(f32[8,1,256,256]{2,3,1,0:T(8,128)S(1)} %get-tuple-element.139, f32[8,1,256,256]{2,3,1,0:T(8,128)S(1)} %get-tuple-element.138), kind=kOutput, calls=%fused_computation.17 | convolution fusion | flops 3223257088 | bytes 8388608 | tf_op jit(solution)/shard_map/ncjk,kl->ncjl/dot_general | solution.py:36
  98.4 5.3 %fusion = f32[8,2,256,256]{2,3,1,0:T(8,128)S(1)} fusion(f32[8,1,256,256]{2,3,1,0:T(8,128)S(1)} %get-tuple-element.139, f32[8,1,256,256]{2,3,1,0:T(8,128)S(1)} %get-tuple-element.138), kind=kOutput, calls=%fused_computation.16 | convolution fusion | flops 3223388160 | bytes 8388608 | tf_op jit(solution)/shard_map/ncjk,kl->ncjl/dot_general | solution.py:37
  104.4 2.3 copy.90
  106.7 2.2 copy.91
  108.9 5.7 %pad_maximum_fusion.3 = f32[2,4,2,256,256]{3,2,4,0,1:T(2,128)} fusion(f32[2,4,1,256,256]{3,2,4,0,1:T(1,128)S(1)} %copy.91, f32[2,4,1,256,256]{3,2,4,0,1:T(1,128)S(1)} %copy.90), kind=kLoop, calls=%fused_computation.15 | loop fusion | flops 1048576 | bytes 8388608 | tf_op jit(solution)/shard_map/stack | solution.py:53
  114.7 122.7 %while.16 = (s32[]{:T(128)}, f32[2,2,256,384]{3,2,1,0:T(8,128)S(1)}, s32[2,4]{1,0:T(2,128)S(1)}, f32[2,4,2,256,256]{3,2,4,0,1:T(2,128)}, s32[]{:T(128)}, /*index...) while((s32[]{:T(128)}, f32[2,2,256,384]{3,2,1,0:T(8,128)S(1)}, ...), condition=%wide.region_2.3_spmd, body=%wide.region_0.2_spmd.sunk | while | flops 393277 | bytes 13107748 | solution.py:80
  115.8 2.7 gather_fusion
  118.5 3.1 %bitcast_add_fusion.2 = f32[2,2,256,256]{2,1,3,0:T(2,128)} fusion(f32[2,2,256,256]{2,1,3,0:T(2,128)} %gather_fusion, f32[2,4,2,256,256]{3,2,4,0,1:T(2,128)} %get-tuple-element.267, s32[]{:T(128)} %get-tuple-element.254), kind=kLoop, calls=%fused_computation.6.clone.1 | loop fusion | flops 262144 | bytes 3145732 | tf_op jit(solution)/shard_map/while/body/eval_jaxpr/vmap()/add | solution.py:73
  121.7 23.4 %while.17 = (s32[]{:T(128)}, f32[2,2,256,384]{3,2,1,0:T(8,128)S(1)}, s32[2,4]{1,0:T(2,128)S(1)}, f32[2,2,256,256]{2,1,3,0:T(2,128)}, s32[]{:T(128)}, /*index=5*/s32[4]{0:T(128)S(1)}, s32[]{:T(128)}) while((s32[]{:T(128)}, f32[2,2,256,384]{3,2,1,0:T(8,128)S(1)}, s32[2,4]{1,0:T(2,128)S(1)}, f32[2,2,256,256]{2,1,3,0:T(2,128)}, s32[]{:T(128)}, ...), condition=%wide.while_cond, body=%wide.while_body.sunk | while | flops 131101 | bytes 4718787 | solution.py:73
  122.4 3.2 %and_reduce_fusion.2 = pred[]{:T(512)} fusion(s32[4]{0:T(128)S(1)} %get-tuple-element.242, s32[1]{0:T(128)} %bitcast.76, s32[1]{0:T(128)} %bitcast.77, s32[1]{0:T(128)} %bitcast.78, s32[1]{0:T(128)} %bitcast.79), kind=kLoop, calls=%fused_computation.3.clone.1 | loop fusion | flops 27 | bytes 33 | tf_op jit(solution)/shard_map/while/body/eval_jaxpr/vmap(vmap())/scatter
  129.1 4.3 %dynamic-update-slice.3 = f32[2,2,256,384]{3,2,1,0:T(8,128)S(1)} dynamic-update-slice(f32[2,2,256,384]{3,2,1,0:T(8,128)S(1)} %get-tuple-element.231, f32[1,2,256,256]{3,2,1,0:T(8,128)S(1)} %dynamic-slice_select_fusion.2, s32[]{:T(128)} %bitcast.74, s32[]{:T(128)} %constant.69.clone.1..sunk.1..sunk, s32[]{:T(128)} %constant.69.clone.1..sunk.1..sunk, s32[]{:T(128)} %bitcast.75) | dynamic-update-slice | bytes 1048580 | tf_op jit(solution)/shard_map/while/body/eval_jaxpr/vmap(vmap())/scatter
  134.1 3.2 %and_reduce_fusion.2 = pred[]{:T(512)} fusion(s32[4]{0:T(128)S(1)} %get-tuple-element.242, s32[1]{0:T(128)} %bitcast.76, s32[1]{0:T(128)} %bitcast.77, s32[1]{0:T(128)} %bitcast.78, s32[1]{0:T(128)} %bitcast.79), kind=kLoop, calls=%fused_computation.3.clone.1 | loop fusion | flops 27 | bytes 33 | tf_op jit(solution)/shard_map/while/body/eval_jaxpr/vmap(vmap())/scatter
  140.8 4.3 %dynamic-update-slice.3 = f32[2,2,256,384]{3,2,1,0:T(8,128)S(1)} dynamic-update-slice(f32[2,2,256,384]{3,2,1,0:T(8,128)S(1)} %get-tuple-element.231, f32[1,2,256,256]{3,2,1,0:T(8,128)S(1)} %dynamic-slice_select_fusion.2, s32[]{:T(128)} %bitcast.74, s32[]{:T(128)} %constant.69.clone.1..sunk.1..sunk, s32[]{:T(128)} %constant.69.clone.1..sunk.1..sunk, s32[]{:T(128)} %bitcast.75) | dynamic-update-slice | bytes 1048580 | tf_op jit(solution)/shard_map/while/body/eval_jaxpr/vmap(vmap())/scatter
  146.3 2.7 gather_fusion
  149.0 3.1 %bitcast_add_fusion.2 = f32[2,2,256,256]{2,1,3,0:T(2,128)} fusion(f32[2,2,256,256]{2,1,3,0:T(2,128)} %gather_fusion, f32[2,4,2,256,256]{3,2,4,0,1:T(2,128)} %get-tuple-element.267, s32[]{:T(128)} %get-tuple-element.254), kind=kLoop, calls=%fused_computation.6.clone.1 | loop fusion | flops 262144 | bytes 3145732 | tf_op jit(solution)/shard_map/while/body/eval_jaxpr/vmap()/add | solution.py:73
  152.2 21.6 %while.17 = (s32[]{:T(128)}, f32[2,2,256,384]{3,2,1,0:T(8,128)S(1)}, s32[2,4]{1,0:T(2,128)S(1)}, f32[2,2,256,256]{2,1,3,0:T(2,128)}, s32[]{:T(128)}, /*index=5*/s32[4]{0:T(128)S(1)}, s32[]{:T(128)}) while((s32[]{:T(128)}, f32[2,2,256,384]{3,2,1,0:T(8,128)S(1)}, s32[2,4]{1,0:T(2,128)S(1)}, f32[2,2,256,256]{2,1,3,0:T(2,128)}, s32[]{:T(128)}, ...), condition=%wide.while_cond, body=%wide.while_body.sunk | while | flops 131101 | bytes 4718787 | solution.py:73
  152.9 3.2 %and_reduce_fusion.2 = pred[]{:T(512)} fusion(s32[4]{0:T(128)S(1)} %get-tuple-element.242, s32[1]{0:T(128)} %bitcast.76, s32[1]{0:T(128)} %bitcast.77, s32[1]{0:T(128)} %bitcast.78, s32[1]{0:T(128)} %bitcast.79), kind=kLoop, calls=%fused_computation.3.clone.1 | loop fusion | flops 27 | bytes 33 | tf_op jit(solution)/shard_map/while/body/eval_jaxpr/vmap(vmap())/scatter
  159.6 3.4 %dynamic-update-slice.3 = f32[2,2,256,384]{3,2,1,0:T(8,128)S(1)} dynamic-update-slice(f32[2,2,256,384]{3,2,1,0:T(8,128)S(1)} %get-tuple-element.231, f32[1,2,256,256]{3,2,1,0:T(8,128)S(1)} %dynamic-slice_select_fusion.2, s32[]{:T(128)} %bitcast.74, s32[]{:T(128)} %constant.69.clone.1..sunk.1..sunk, s32[]{:T(128)} %constant.69.clone.1..sunk.1..sunk, s32[]{:T(128)} %bitcast.75) | dynamic-update-slice | bytes 1048580 | tf_op jit(solution)/shard_map/while/body/eval_jaxpr/vmap(vmap())/scatter
  163.7 3.2 %and_reduce_fusion.2 = pred[]{:T(512)} fusion(s32[4]{0:T(128)S(1)} %get-tuple-element.242, s32[1]{0:T(128)} %bitcast.76, s32[1]{0:T(128)} %bitcast.77, s32[1]{0:T(128)} %bitcast.78, s32[1]{0:T(128)} %bitcast.79), kind=kLoop, calls=%fused_computation.3.clone.1 | loop fusion | flops 27 | bytes 33 | tf_op jit(solution)/shard_map/while/body/eval_jaxpr/vmap(vmap())/scatter
  170.4 3.4 %dynamic-update-slice.3 = f32[2,2,256,384]{3,2,1,0:T(8,128)S(1)} dynamic-update-slice(f32[2,2,256,384]{3,2,1,0:T(8,128)S(1)} %get-tuple-element.231, f32[1,2,256,256]{3,2,1,0:T(8,128)S(1)} %dynamic-slice_select_fusion.2, s32[]{:T(128)} %bitcast.74, s32[]{:T(128)} %constant.69.clone.1..sunk.1..sunk, s32[]{:T(128)} %constant.69.clone.1..sunk.1..sunk, s32[]{:T(128)} %bitcast.75) | dynamic-update-slice | bytes 1048580 | tf_op jit(solution)/shard_map/while/body/eval_jaxpr/vmap(vmap())/scatter
  175.0 2.7 gather_fusion
  177.7 3.1 %bitcast_add_fusion.2 = f32[2,2,256,256]{2,1,3,0:T(2,128)} fusion(f32[2,2,256,256]{2,1,3,0:T(2,128)} %gather_fusion, f32[2,4,2,256,256]{3,2,4,0,1:T(2,128)} %get-tuple-element.267, s32[]{:T(128)} %get-tuple-element.254), kind=kLoop, calls=%fused_computation.6.clone.1 | loop fusion | flops 262144 | bytes 3145732 | tf_op jit(solution)/shard_map/while/body/eval_jaxpr/vmap()/add | solution.py:73
  180.9 24.7 %while.17 = (s32[]{:T(128)}, f32[2,2,256,384]{3,2,1,0:T(8,128)S(1)}, s32[2,4]{1,0:T(2,128)S(1)}, f32[2,2,256,256]{2,1,3,0:T(2,128)}, s32[]{:T(128)}, /*index=5*/s32[4]{0:T(128)S(1)}, s32[]{:T(128)}) while((s32[]{:T(128)}, f32[2,2,256,384]{3,2,1,0:T(8,128)S(1)}, s32[2,4]{1,0:T(2,128)S(1)}, f32[2,2,256,256]{2,1,3,0:T(2,128)}, s32[]{:T(128)}, ...), condition=%wide.while_cond, body=%wide.while_body.sunk | while | flops 131101 | bytes 4718787 | solution.py:73
  181.6 3.2 %and_reduce_fusion.2 = pred[]{:T(512)} fusion(s32[4]{0:T(128)S(1)} %get-tuple-element.242, s32[1]{0:T(128)} %bitcast.76, s32[1]{0:T(128)} %bitcast.77, s32[1]{0:T(128)} %bitcast.78, s32[1]{0:T(128)} %bitcast.79), kind=kLoop, calls=%fused_computation.3.clone.1 | loop fusion | flops 27 | bytes 33 | tf_op jit(solution)/shard_map/while/body/eval_jaxpr/vmap(vmap())/scatter
  188.3 5.0 %dynamic-update-slice.3 = f32[2,2,256,384]{3,2,1,0:T(8,128)S(1)} dynamic-update-slice(f32[2,2,256,384]{3,2,1,0:T(8,128)S(1)} %get-tuple-element.231, f32[1,2,256,256]{3,2,1,0:T(8,128)S(1)} %dynamic-slice_select_fusion.2, s32[]{:T(128)} %bitcast.74, s32[]{:T(128)} %constant.69.clone.1..sunk.1..sunk, s32[]{:T(128)} %constant.69.clone.1..sunk.1..sunk, s32[]{:T(128)} %bitcast.75) | dynamic-update-slice | bytes 1048580 | tf_op jit(solution)/shard_map/while/body/eval_jaxpr/vmap(vmap())/scatter
  193.9 3.2 %and_reduce_fusion.2 = pred[]{:T(512)} fusion(s32[4]{0:T(128)S(1)} %get-tuple-element.242, s32[1]{0:T(128)} %bitcast.76, s32[1]{0:T(128)} %bitcast.77, s32[1]{0:T(128)} %bitcast.78, s32[1]{0:T(128)} %bitcast.79), kind=kLoop, calls=%fused_computation.3.clone.1 | loop fusion | flops 27 | bytes 33 | tf_op jit(solution)/shard_map/while/body/eval_jaxpr/vmap(vmap())/scatter
  200.6 5.0 %dynamic-update-slice.3 = f32[2,2,256,384]{3,2,1,0:T(8,128)S(1)} dynamic-update-slice(f32[2,2,256,384]{3,2,1,0:T(8,128)S(1)} %get-tuple-element.231, f32[1,2,256,256]{3,2,1,0:T(8,128)S(1)} %dynamic-slice_select_fusion.2, s32[]{:T(128)} %bitcast.74, s32[]{:T(128)} %constant.69.clone.1..sunk.1..sunk, s32[]{:T(128)} %constant.69.clone.1..sunk.1..sunk, s32[]{:T(128)} %bitcast.75) | dynamic-update-slice | bytes 1048580 | tf_op jit(solution)/shard_map/while/body/eval_jaxpr/vmap(vmap())/scatter
  206.7 2.7 gather_fusion
  209.4 3.1 %bitcast_add_fusion.2 = f32[2,2,256,256]{2,1,3,0:T(2,128)} fusion(f32[2,2,256,256]{2,1,3,0:T(2,128)} %gather_fusion, f32[2,4,2,256,256]{3,2,4,0,1:T(2,128)} %get-tuple-element.267, s32[]{:T(128)} %get-tuple-element.254), kind=kLoop, calls=%fused_computation.6.clone.1 | loop fusion | flops 262144 | bytes 3145732 | tf_op jit(solution)/shard_map/while/body/eval_jaxpr/vmap()/add | solution.py:73
  212.6 24.7 %while.17 = (s32[]{:T(128)}, f32[2,2,256,384]{3,2,1,0:T(8,128)S(1)}, s32[2,4]{1,0:T(2,128)S(1)}, f32[2,2,256,256]{2,1,3,0:T(2,128)}, s32[]{:T(128)}, /*index=5*/s32[4]{0:T(128)S(1)}, s32[]{:T(128)}) while((s32[]{:T(128)}, f32[2,2,256,384]{3,2,1,0:T(8,128)S(1)}, s32[2,4]{1,0:T(2,128)S(1)}, f32[2,2,256,256]{2,1,3,0:T(2,128)}, s32[]{:T(128)}, ...), condition=%wide.while_cond, body=%wide.while_body.sunk | while | flops 131101 | bytes 4718787 | solution.py:73
  213.3 3.2 %and_reduce_fusion.2 = pred[]{:T(512)} fusion(s32[4]{0:T(128)S(1)} %get-tuple-element.242, s32[1]{0:T(128)} %bitcast.76, s32[1]{0:T(128)} %bitcast.77, s32[1]{0:T(128)} %bitcast.78, s32[1]{0:T(128)} %bitcast.79), kind=kLoop, calls=%fused_computation.3.clone.1 | loop fusion | flops 27 | bytes 33 | tf_op jit(solution)/shard_map/while/body/eval_jaxpr/vmap(vmap())/scatter
  220.0 5.0 %dynamic-update-slice.3 = f32[2,2,256,384]{3,2,1,0:T(8,128)S(1)} dynamic-update-slice(f32[2,2,256,384]{3,2,1,0:T(8,128)S(1)} %get-tuple-element.231, f32[1,2,256,256]{3,2,1,0:T(8,128)S(1)} %dynamic-slice_select_fusion.2, s32[]{:T(128)} %bitcast.74, s32[]{:T(128)} %constant.69.clone.1..sunk.1..sunk, s32[]{:T(128)} %constant.69.clone.1..sunk.1..sunk, s32[]{:T(128)} %bitcast.75) | dynamic-update-slice | bytes 1048580 | tf_op jit(solution)/shard_map/while/body/eval_jaxpr/vmap(vmap())/scatter
  225.7 3.2 %and_reduce_fusion.2 = pred[]{:T(512)} fusion(s32[4]{0:T(128)S(1)} %get-tuple-element.242, s32[1]{0:T(128)} %bitcast.76, s32[1]{0:T(128)} %bitcast.77, s32[1]{0:T(128)} %bitcast.78, s32[1]{0:T(128)} %bitcast.79), kind=kLoop, calls=%fused_computation.3.clone.1 | loop fusion | flops 27 | bytes 33 | tf_op jit(solution)/shard_map/while/body/eval_jaxpr/vmap(vmap())/scatter
  232.4 5.0 %dynamic-update-slice.3 = f32[2,2,256,384]{3,2,1,0:T(8,128)S(1)} dynamic-update-slice(f32[2,2,256,384]{3,2,1,0:T(8,128)S(1)} %get-tuple-element.231, f32[1,2,256,256]{3,2,1,0:T(8,128)S(1)} %dynamic-slice_select_fusion.2, s32[]{:T(128)} %bitcast.74, s32[]{:T(128)} %constant.69.clone.1..sunk.1..sunk, s32[]{:T(128)} %constant.69.clone.1..sunk.1..sunk, s32[]{:T(128)} %bitcast.75) | dynamic-update-slice | bytes 1048580 | tf_op jit(solution)/shard_map/while/body/eval_jaxpr/vmap(vmap())/scatter
  240.2 5.5 %collective-permute-start.3 = (f32[2,2,256,128]{3,1,0,2:T(2,128)S(1)}, f32[2,2,256,128]{3,1,0,2:T(2,128)S(1)}, u32[]{:S(2)}, u32[]{:S(2)}) collective-permute-start(f32[2,2,256,128]{3,1,0,2:T(2,128)S(1)} %get-tuple-element.147), channel_id=1, source_target_pairs={{0,1},{1,2},{2,3},{3,4},{4,5},{5,6},{6,7},{7,8},{8,9},{9,10},{10,1... | collective-permute-start | bytes 1572872 | tf_op jit(solution)/shard_map/ppermute | solution.py:14
  245.8 8.4 %collective-permute-done.2 = f32[2,2,256,128]{3,1,0,2:T(2,128)S(1)} collective-permute-done((f32[2,2,256,128]{3,1,0,2:T(2,128)S(1)}, f32[2,2,256,128]{3,1,0,2:T(2,128)S(1)}, u32[]{:S(2)}, u32[]{:S(2)}) %collective-permute-start.2) | collective-permute-done | bytes 524320 | tf_op jit(solution)/shard_map/ppermute | solution.py:14
  255.5 36.6 %all_to_all.15 = f32[1,2,2,256,128]{4,2,1,0,3:T(2,128)S(1)} all-to-all(f32[1,2,2,256,128]{4,2,1,0,3:T(2,128)S(1)} %fusion.15), channel_id=1, replica_groups=mesh['grp'=4,'scan'=32] {'grp','scan'}, dimensions={3} | all-to-all | bytes 1048576 | tf_op jit(solution)/shard_map/all_to_all | solution.py:118
  (89 shorter events, 53.5 us)
Async XLA Ops:
  1.3 16.1 %collective-permute-start = (f32[2,2,256,128]{2,1,0,3:T(2,128)S(1)}, f32[2,2,256,128]{2,1,0,3:T(2,128)S(1)}, u32[]{:S(2)}, u32[]{:S(2)}) collective-permute-start(f32[2,2,256,128]{2,1,0,3:T(2,128)S(1)} %copy.74), channel_id=1, source_target_pairs={{0,1},{1,2},{2,3},{3,4},{4,5},{5,6},{6,7},{7,8},{8,9},{9,10},{10,1... | collective-permute-start | bytes 1572872 | tf_op jit(solution)/shard_map/ppermute | solution.py:14
  6.8 23.9 %collective-permute-start.1 = (f32[2,2,256,128]{2,1,0,3:T(2,128)S(1)}, f32[2,2,256,128]{2,1,0,3:T(2,128)}, u32[]{:S(2)}, u32[]{:S(2)}) collective-permute-start(f32[2,2,256,128]{2,1,0,3:T(2,128)S(1)} %copy.74), channel_id=1, source_target_pairs={{1,0},{2,1},{3,2},{4,3},{5,4},{6,5},{7,6},{8,7},{9,8},{10,9},{11,1... | collective-permute-start | bytes 1572872 | tf_op jit(solution)/shard_map/ppermute | solution.py:14
  66.0 8.7 %copy-start = (f32[2,4,256,256]{3,2,1,0:T(8,128)S(1)}, f32[2,4,256,256]{3,2,1,0:T(8,128)}, u32[]{:S(2)}) copy-start(f32[2,4,256,256]{3,2,1,0:T(8,128)} %param.8) | copy-start | bytes 6291460
  108.9 5.8 %copy-start.1 = (s32[4]{0:T(128)S(1)}, s32[4]{0:T(128)}, u32[]{:S(2)}) copy-start(s32[4]{0:T(128)} %constant.323) | copy-start | bytes 52
  108.9 5.8 %copy-start.2 = (s32[3]{0:T(128)S(1)}, s32[3]{0:T(128)}, u32[]{:S(2)}) copy-start(s32[3]{0:T(128)} %constant.67.clone.1) | copy-start | bytes 40
  238.9 15.3 %collective-permute-start.2 = (f32[2,2,256,128]{3,1,0,2:T(2,128)S(1)}, f32[2,2,256,128]{3,1,0,2:T(2,128)S(1)}, u32[]{:S(2)}, u32[]{:S(2)}) collective-permute-start(f32[2,2,256,128]{3,1,0,2:T(2,128)S(1)} %get-tuple-element.146), channel_id=1, source_target_pairs={{1,0},{2,1},{3,2},{4,3},{5,4},{6,5},{7,6},{8,7},{9,8},{10,9},{11,1... | collective-permute-start | bytes 1572872 | tf_op jit(solution)/shard_map/ppermute | solution.py:14
  240.2 14.9 %collective-permute-start.3 = (f32[2,2,256,128]{3,1,0,2:T(2,128)S(1)}, f32[2,2,256,128]{3,1,0,2:T(2,128)S(1)}, u32[]{:S(2)}, u32[]{:S(2)}) collective-permute-start(f32[2,2,256,128]{3,1,0,2:T(2,128)S(1)} %get-tuple-element.147), channel_id=1, source_target_pairs={{0,1},{1,2},{2,3},{3,4},{4,5},{5,6},{6,7},{7,8},{8,9},{9,10},{10,1... | collective-permute-start | bytes 1572872 | tf_op jit(solution)/shard_map/ppermute | solution.py:14
where the time goes:
time: 298 us; the launch traced here: 293 us
  local copies, waits for them, and re-layouts  91.3 us (31%)
  other arithmetic  67.6 us (23%)
  matrix products  53.7 us (18%)
  blocking collectives  36.6 us (12%)
  waiting for transfers between devices  29.8 us (10%)
  starting transfers between devices  13.6 us (5%)
    scatter x40, local copies, waits for them, and re-layouts  52.2 us
    scatter x16, other arithmetic  41.9 us
    all_to_all x1, blocking collectives, per_device(): lax.all_to_all(tile_sum[None], ('grp', 'scan'), split_axis=3, concat_axis...  36.6 us
    ppermute x4, waiting for transfers between devices, passed_along(): lax.ppermute(value, axis, [(source, source + steps) for source in range(f...  29.8 us
    dot_general x2, matrix products, transform(): jnp.einsum('ncjk,kl->ncjl', middle, table_real, precision=highest)  14 us
    dot_general x2, matrix products, transform(): jnp.einsum('ncjk,kl->ncjl', middle, table_imag, precision=highest)  14 us
    ppermute x4, starting transfers between devices, passed_along(): lax.ppermute(value, axis, [(source, source + steps) for source in range(f...  13.6 us
    dot_general x2, matrix products, transform(): jnp.einsum('ij,ncjk->ncik', table_imag, field, precision=highest)  12.9 us
  transfers between devices with their start and end apart: 4, of which 4 were waited for; matrix products, arithmetic and copies ran while one was open for 1% of the time, Pallas kernels for 0%

commit v1 on v0

v1 whole, which is shorter than its diff:
```python
import functools
import math

import jax
import jax.numpy as jnp
import ml_dtypes
import numpy as np
from jax import lax
from jax.experimental import pallas as pl
from jax.experimental.pallas import tpu as pltpu
from jax.sharding import PartitionSpec as P

BF = jnp.bfloat16
F32 = jnp.float32
MESH = pl.DeviceIdType.MESH
GRP, SCAN = 4, 32
DEVS = GRP * SCAN
YZ = 16


def tables():
    n = np.arange(128)
    mats = []
    for odd in (0, 1):
        k = (np.arange(128) + 64 * odd) % 128
        angle = 2 * math.pi * ((n[None, :] * (2 * k[:, None] + odd)) % 256) / 256
        c, s = np.cos(angle) / 16, np.sin(angle) / 16
        forward = np.block([[c, s], [-s, c]])
        mats += [forward, forward.T]
    t = np.stack(mats)
    hi = t.astype(np.float32).astype(ml_dtypes.bfloat16)
    lo = (t - hi.astype(np.float64)).astype(np.float32).astype(ml_dtypes.bfloat16)
    return np.stack([hi, lo], 1)


def split(x):
    hi = x.astype(BF)
    return hi, (x - hi.astype(F32)).astype(BF)


def dot(a, b):
    return jnp.dot(a, b, preferred_element_type=F32)


def left(t_ref, i, x):
    hi, lo = split(x)
    return dot(t_ref[i, 0], hi) + dot(t_ref[i, 1], hi) + dot(t_ref[i, 0], lo)


def right(x, t_ref, i):
    hi, lo = split(x)
    return dot(hi, t_ref[i, 0]) + dot(lo, t_ref[i, 0]) + dot(hi, t_ref[i, 1])


def rolled_probe(ill_ref, d, c):
    lane = lax.broadcasted_iota(jnp.int32, (256, 128), 1)
    shift = lax.rem(d, 128)
    r0 = pltpu.roll(ill_ref[c, :, 0:128], shift, 1)
    r1 = pltpu.roll(ill_ref[c, :, 128:256], shift, 1)
    return jnp.where(lane < d, r0, r1), jnp.where(lane < d, r1, r0)


def ordered_amplitude(amp_ref, a, p):
    lane = lax.broadcasted_iota(jnp.int32, (128, 128), 1)
    first = lane < 64
    ia = jnp.where(first, 2 * lane, 2 * lane - 127)
    ib = jnp.where(first, 2 * lane + 1, 2 * lane - 128)
    even, odd = [], []
    for k in (0, 1):
        x = amp_ref[a, p, 0, pl.ds(k, 128, stride=2), :]
        y = amp_ref[a, p, 1, pl.ds(k, 128, stride=2), :]
        if k:
            x = jnp.concatenate([x[64:], x[:64]], 0)
            y = jnp.concatenate([y[64:], y[:64]], 0)
        x = jnp.take_along_axis(x, ia, axis=1, mode="promise_in_bounds")
        y = jnp.take_along_axis(y, ib, axis=1, mode="promise_in_bounds")
        even.append(jnp.where(first, x, y))
        odd.append(jnp.where(first, y, x))
    return jnp.concatenate(even, 0), jnp.concatenate(odd, 0)


def residual(f, amp):
    re, im = f[:, :128], f[:, 128:]
    w = 1.0 - amp * lax.rsqrt(jnp.maximum(re * re + im * im, 0.25))
    return jnp.concatenate([re * w, im * w], 1)


def patch(a, p, d, t_ref, ill_ref, amp_ref, tiles, acc):
    lane = lax.broadcasted_iota(jnp.int32, (256, 128), 1)
    m = lane < d
    ilr, irr = rolled_probe(ill_ref, d, 0)
    ili, iri = rolled_probe(ill_ref, d, 1)
    tl_r, tl_i = tiles[1, a, 0], tiles[1, a, 1]
    tr_r = jnp.where(m, tiles[2, a, 0], tiles[0, a, 0])
    tr_i = jnp.where(m, tiles[2, a, 1], tiles[0, a, 1])
    wr = jnp.concatenate([ilr * tl_r - ili * tl_i, irr * tr_r - iri * tr_i], 1)
    wi = jnp.concatenate([ilr * tl_i + ili * tl_r, irr * tr_i + iri * tr_r], 1)
    amp_even, amp_odd = ordered_amplitude(amp_ref, a, p)
    e = left(t_ref, 0, jnp.concatenate([wr[:128] + wr[128:], wi[:128] + wi[128:]], 0))
    o = left(t_ref, 2, jnp.concatenate([wr[:128] - wr[128:], wi[:128] - wi[128:]], 0))
    xr = jnp.concatenate([e[:128], o[:128]], 0)
    xi = jnp.concatenate([e[128:], o[128:]], 0)
    u = jnp.concatenate([xr[:, :128] + xr[:, 128:], xi[:, :128] + xi[:, 128:]], 1)
    v = jnp.concatenate([xr[:, :128] - xr[:, 128:], xi[:, :128] - xi[:, 128:]], 1)
    de = residual(right(u, t_ref, 1), amp_even)
    do = residual(right(v, t_ref, 3), amp_odd)
    be = right(de, t_ref, 0)
    bo = right(do, t_ref, 2)
    lh, rh = be + bo, be - bo
    yr = jnp.concatenate([lh[:, :128], rh[:, :128]], 1)
    yi = jnp.concatenate([lh[:, 128:], rh[:, 128:]], 1)
    e = left(t_ref, 1, jnp.concatenate([yr[:128], yi[:128]], 0))
    o = left(t_ref, 3, jnp.concatenate([yr[128:], yi[128:]], 0))
    top, bottom = e + o, e - o
    br = jnp.concatenate([top[:128], bottom[:128]], 0)
    bi = jnp.concatenate([top[128:], bottom[128:]], 0)
    acc[1, 0] += ilr * br[:, :128] + ili * bi[:, :128]
    acc[1, 1] += ilr * bi[:, :128] - ili * br[:, :128]
    gr_r = irr * br[:, 128:] + iri * bi[:, 128:]
    gr_i = irr * bi[:, 128:] - iri * br[:, 128:]
    acc[2, 0] += jnp.where(m, gr_r, 0.0)
    acc[2, 1] += jnp.where(m, gr_i, 0.0)
    acc[0, 0] += jnp.where(m, 0.0, gr_r)
    acc[0, 1] += jnp.where(m, 0.0, gr_i)


def kernel(
    off_ref, t_hbm, ill_hbm, amp_hbm, proj_hbm, out_ref,
    tab, ill, amp, tiles, acc, send, recv,
    local_sem, pair_send, pair_recv, fwd_send, fwd_recv, all_send, all_recv, own_sem, ready,
):
    g, s = lax.axis_index("grp"), lax.axis_index("scan")
    me = g * SCAN + s
    yz, odd = s // 2, s % 2
    local = [
        pltpu.make_async_copy(proj_hbm, tiles.at[1], local_sem.at[0]),
        pltpu.make_async_copy(ill_hbm, ill, local_sem.at[1]),
        pltpu.make_async_copy(t_hbm, tab, local_sem.at[2]),
        pltpu.make_async_copy(amp_hbm.at[:, :, :, pl.ds(0, 128)], amp.at[:, :, 0], local_sem.at[3]),
        pltpu.make_async_copy(amp_hbm.at[:, :, :, pl.ds(128, 128)], amp.at[:, :, 1], local_sem.at[4]),
    ]
    for c in local:
        c.start()

    barrier = pltpu.get_barrier_semaphore()
    row = g * 2 + odd
    for k in range(1, 8):
        other = (row + k) % 8
        pl.semaphore_signal(
            barrier, inc=1, device_id={"grp": other // 2, "scan": yz * 2 + other % 2}, device_id_type=MESH
        )
    for k in range(1, YZ):
        pl.semaphore_signal(
            barrier, inc=1, device_id={"grp": g, "scan": (yz + k) % YZ * 2 + odd}, device_id_type=MESH
        )
    pl.semaphore_wait(barrier, 7 + YZ - 1)

    near = 2 - 2 * odd
    local[0].wait()
    chunks = [(a, c) for a in range(2) for c in range(2)]

    def pair_copy(i):
        a, c = chunks[i]
        return pltpu.make_async_remote_copy(
            proj_hbm.at[a, c], tiles.at[2 * odd, a, c], pair_send.at[i], pair_recv.at[i],
            device_id={"grp": g, "scan": s + 1 - 2 * odd}, device_id_type=MESH,
        )

    def fwd_copy(i):
        a, c = chunks[i]
        return pltpu.make_async_remote_copy(
            tiles.at[near, a, c], tiles.at[2 * odd, a, c], fwd_send.at[i], fwd_recv.at[i],
            device_id={"grp": g, "scan": s + 2 - 4 * odd}, device_id_type=MESH,
        )

    for i in range(4):
        pair_copy(i).start()
    for k in range(1, YZ):
        pl.semaphore_signal(
            ready, inc=1, device_id={"grp": g, "scan": (yz + k) % YZ * 2 + odd}, device_id_type=MESH
        )
    sends_on = jnp.logical_and(s != SCAN - 2, s != 1)
    gets = jnp.logical_and(s != 0, s != SCAN - 1)

    @pl.when(jnp.logical_not(gets))
    def _():
        tiles[2 * odd] = jnp.zeros_like(tiles[0])

    for c in local[1:]:
        c.wait()

    def all_copy(a, k):
        to = (me + k) % DEVS
        return pltpu.make_async_remote_copy(
            send.at[a, to], recv.at[a, me], all_send.at[a], all_recv.at[a],
            device_id={"grp": to // SCAN, "scan": to % SCAN}, device_id_type=MESH,
        )

    for a in range(2):
        for i in (2 * a, 2 * a + 1):
            pair_copy(i).wait_recv()

            @pl.when(sends_on)
            def _():
                fwd_copy(i).start()

        for i in (2 * a, 2 * a + 1):

            @pl.when(gets)
            def _():
                fwd_copy(i).wait_recv()

        acc[...] = jnp.zeros_like(acc)

        def one(p, carry):
            patch(a, p, off_ref[a, p], tab, ill, amp, tiles, acc)
            return carry

        lax.fori_loop(0, 4, one, 0)

        def pack(q, carry):
            for u in range(4):
                to = q * 4 + u
                for t in range(3):
                    for c in range(2):
                        send[a, to, t, 2 * c : 2 * c + 2, :] = acc[t, c, pl.ds(to * 2, 2), :]
            return carry

        lax.fori_loop(0, DEVS // 4, pack, 0)
        if a == 0:
            pl.semaphore_wait(ready, YZ - 1)
        pltpu.make_async_copy(send.at[a, me], recv.at[a, me], own_sem.at[a]).start()

        def post(k, carry):
            all_copy(a, k).start()
            return carry

        lax.fori_loop(1, DEVS, post, 0)

    for i in range(4):
        pair_copy(i).wait_send()

        @pl.when(sends_on)
        def _():
            fwd_copy(i).wait_send()

    for a in range(2):
        pltpu.make_async_copy(send.at[a, me], recv.at[a, me], own_sem.at[a]).wait()
        bulk = pltpu.make_async_remote_copy(
            send.at[a, pl.ds(0, DEVS - 1)], recv.at[a, pl.ds(0, DEVS - 1)], all_send.at[a], all_recv.at[a],
            device_id={"grp": g, "scan": s + 1 - 2 * odd}, device_id_type=MESH,
        )
        bulk.wait_recv()

        def gather(h, carry):
            for t in range(SCAN):
                total = None
                for k in range(3):
                    src = t + 1 - k
                    if 0 <= src < SCAN:
                        x = recv[a, h * SCAN + src, k]
                        total = x if total is None else total + x
                for c in range(2):
                    out_ref[2 * h + a, c, :, 128 * t : 128 * t + 128] = total[2 * c : 2 * c + 2]
            return carry

        lax.fori_loop(0, GRP, gather, 0)
        bulk.wait_send()


def per_device(projection, illumination, amplitude, offsets):
    s = lax.axis_index("scan")
    d = offsets - (s * 128 - 128)
    return pl.pallas_call(
        kernel,
        out_shape=jax.ShapeDtypeStruct((8, 2, 2, 4096), F32),
        in_specs=[pl.BlockSpec(memory_space=pltpu.SMEM)] + [pl.BlockSpec(memory_space=pl.ANY)] * 4,
        out_specs=pl.BlockSpec(memory_space=pltpu.VMEM),
        scratch_shapes=[
            pltpu.VMEM((4, 2, 256, 256), BF),
            pltpu.VMEM((2, 256, 256), F32),
            pltpu.VMEM((2, 4, 2, 256, 128), F32),
            pltpu.VMEM((3, 2, 2, 256, 128), F32),
            pltpu.VMEM((3, 2, 256, 128), F32),
            pltpu.VMEM((2, DEVS, 3, 4, 128), F32),
            pltpu.VMEM((2, DEVS, 3, 4, 128), F32),
            pltpu.SemaphoreType.DMA((5,)),
            pltpu.SemaphoreType.DMA((4,)),
            pltpu.SemaphoreType.DMA((4,)),
            pltpu.SemaphoreType.DMA((4,)),
            pltpu.SemaphoreType.DMA((4,)),
            pltpu.SemaphoreType.DMA((2,)),
            pltpu.SemaphoreType.DMA((2,)),
            pltpu.SemaphoreType.DMA((2,)),
            pltpu.SemaphoreType.REGULAR,
        ],
        compiler_params=pltpu.CompilerParams(
            collective_id=0, has_side_effects=True, vmem_limit_bytes=48 << 20
        ),
        name="gradient",
    )(d, jnp.asarray(tables()), illumination, amplitude, projection)


def solution(mesh):
    placed = (P("grp", None, None, "scan"), P(), P("grp", "scan", None, None), P("grp", "scan"))
    return jax.shard_map(
        per_device,
        mesh=mesh,
        in_specs=placed,
        out_specs=P(None, None, ("grp", "scan"), None),
        check_vma=False,
    )
```

time: 298 us -> 71.8 us (0.24); the launches traced: 293 us -> 70.7 us
  local copies, waits for them, and re-layouts: 91.3 us -> 5.69 us
  other arithmetic: 67.6 us -> 0.68 us
  Pallas kernels: 0 us -> 64.3 us
  matrix products: 53.7 us -> 0 us
  blocking collectives: 36.6 us -> 0 us
  waiting for transfers between devices: 29.8 us -> 0 us
  starting transfers between devices: 13.6 us -> 0 us
    pallas_call x0 -> x1, Pallas kernels: none -> 64.3 us  [per_device(): pl.pallas_call(kernel, out_shape=jax.ShapeDtypeStruct((8, 2, 2, 4096), F3...]
    dot_general x8 -> x0, matrix products: 53.7 us -> none  [the longest x2 14 us: transform(): jnp.einsum('ncjk,kl->ncjl', middle, table_real, precision=highest)]
    scatter x40 -> x0, local copies, waits for them, and re-layouts: 52.2 us -> none
    scatter x20 -> x0, other arithmetic: 42.2 us -> none
    all_to_all x1 -> x0, blocking collectives: 36.6 us -> none  [per_device(): lax.all_to_all(tile_sum[None], ('grp', 'scan'), split_axis=3, concat_axis...]
    ppermute x4 -> x0, waiting for transfers between devices: 29.8 us -> none  [passed_along(): lax.ppermute(value, axis, [(source, source + steps) for source in range(f...]
    gather x6 -> x0, local copies, waits for them, and re-layouts: 17.8 us -> none  [the longest x4 10.8 us: add_patch(): current = lax.dynamic_slice_in_dim(angle_sum, start_col, width, 2)]
    ppermute x4 -> x0, starting transfers between devices: 13.6 us -> none  [passed_along(): lax.ppermute(value, axis, [(source, source + steps) for source in range(f...]
  transfers between devices with their start and end apart: 4 -> 0, of which waited for: 4 -> 0; matrix products, arithmetic and copies ran while one was open for 1% -> 0% of each run, Pallas kernels for 0% -> 0%
where the time goes in v1:
time: 71.8 us; the launch traced here: 70.7 us
  Pallas kernels  64.3 us (90%)
  local copies, waits for them, and re-layouts  5.69 us (8%)
    pallas_call x1, Pallas kernels, per_device(): pl.pallas_call(kernel, out_shape=jax.ShapeDtypeStruct((8, 2, 2, 4096), F3...  64.3 us
    unnamed x9, local copies, waits for them, and re-layouts  5.69 us

profile of v1, /device:TPU:1, one launch (start us, length us, event | category | flops | bytes accessed | tf_op | source)
XLA Modules:
  0.0 70.7 jit_solution(15929712270842374637)
XLA Ops:
  0.0 0.7 broadcast_subtract_fusion.off_ref
  0.7 0.0 copy-start
  0.7 1.6 %copy-done = f32[2,4,256,256]{3,2,1,0:T(8,128)S(1)} copy-done((f32[2,4,256,256]{3,2,1,0:T(8,128)S(1)}, f32[2,4,256,256]{3,2,1,0:T(8,128)}, u32[]{:S(2)}) %copy-start) | copy-done | bytes 2097176
  2.3 0.0 copy-start.1
  2.3 1.2 %copy-done.1 = bf16[4,2,256,256]{3,2,1,0:T(8,128)(2,1)S(1)} copy-done((bf16[4,2,256,256]{3,2,1,0:T(8,128)(2,1)S(1)}, bf16[4,2,256,256]{3,2,1,0:T(8,128)(2,1)}, u32[]{:S(2)}) %copy-start.1) | copy-done | bytes 1048600
  3.5 0.0 copy-start.2
  3.5 1.0 %copy-done.2 = f32[2,256,256]{2,1,0:T(8,128)S(1)} copy-done((f32[2,256,256]{2,1,0:T(8,128)S(1)}, f32[2,256,256]{2,1,0:T(8,128)}, u32[]{:S(2)}) %copy-start.2) | copy-done | bytes 524312
  4.5 0.0 copy-start.3
  4.5 1.0 %copy-done.3 = f32[2,2,256,128]{3,2,1,0:T(8,128)S(1)} copy-done((f32[2,2,256,128]{3,2,1,0:T(8,128)S(1)}, f32[2,2,256,128]{3,2,1,0:T(8,128)}, u32[]{:S(2)}) %copy-start.3) | copy-done | bytes 524312
  5.6 64.3 %gradient.1 = f32[8,2,2,4096]{3,2,1,0:T(2,128)S(1)} custom-call(s32[2,4]{1,0:T(2,128)S(1)} %broadcast_subtract_fusion.off_ref, bf16[4,2,256,256]{3,2,1,0:T(8,128)(2,1)S(1)} %copy-done.1, f32[2,256,256]{2,1,0:T(8,128)S(1)} %copy-done.2, f32[2,4,256,256]{3,2,1,0:T(8,128)S(1)} %copy-done, f32[2,2,256,128]{3,2,1,0:T(8,128)S(1)} %copy-done.3), custom_call_target="tpu_custom_call" | custom-call | tf_op jit(solution)/shard_map/gradient/pallas_call | solution.py:274
  69.9 0.8 %copy.7 = f32[8,2,2,4096]{3,2,1,0:T(2,128)} copy(f32[8,2,2,4096]{3,2,1,0:T(2,128)S(1)} %gradient.1) | data formatting | bytes 1048576
Async XLA Ops:
  0.7 1.6 %copy-start = (f32[2,4,256,256]{3,2,1,0:T(8,128)S(1)}, f32[2,4,256,256]{3,2,1,0:T(8,128)}, u32[]{:S(2)}) copy-start(f32[2,4,256,256]{3,2,1,0:T(8,128)} %amp_hbm.1) | copy-start | bytes 6291460
  2.3 1.2 %copy-start.1 = (bf16[4,2,256,256]{3,2,1,0:T(8,128)(2,1)S(1)}, bf16[4,2,256,256]{3,2,1,0:T(8,128)(2,1)}, u32[]{:S(2)}) copy-start(bf16[4,2,256,256]{3,2,1,0:T(8,128)(2,1)} %constant.10.clone.t_hbm) | copy-start | bytes 3145732
  3.5 1.0 %copy-start.2 = (f32[2,256,256]{2,1,0:T(8,128)S(1)}, f32[2,256,256]{2,1,0:T(8,128)}, u32[]{:S(2)}) copy-start(f32[2,256,256]{2,1,0:T(8,128)} %ill_hbm.1) | copy-start | bytes 1572868
  4.5 1.0 %copy-start.3 = (f32[2,2,256,128]{3,2,1,0:T(8,128)S(1)}, f32[2,2,256,128]{3,2,1,0:T(8,128)}, u32[]{:S(2)}) copy-start(f32[2,2,256,128]{3,2,1,0:T(8,128)} %proj_hbm.1) | copy-start | bytes 1572868

commit v2 on v1

v2 whole, which is shorter than its diff:
```python
import math

import jax
import jax.numpy as jnp
import ml_dtypes
import numpy as np
from jax import lax
from jax.experimental import pallas as pl
from jax.experimental.pallas import tpu as pltpu
from jax.sharding import PartitionSpec as P

BF = jnp.bfloat16
F32 = jnp.float32
MESH = pl.DeviceIdType.MESH
GRP, SCAN = 4, 32
DEVS = GRP * SCAN
YZ = 16
VMEM_LIMIT = 53 << 20


def tables():
    n = np.arange(128)
    mats = []
    for odd in (0, 1):
        k = (np.arange(128) + 64 * odd) % 128
        angle = 2 * math.pi * ((n[None, :] * (2 * k[:, None] + odd)) % 256) / 256
        c, s = np.cos(angle) / 16, np.sin(angle) / 16
        forward = np.block([[c, s], [-s, c]])
        mats += [forward, forward.T]
    t = np.stack(mats)
    hi = t.astype(np.float32).astype(ml_dtypes.bfloat16)
    lo = (t - hi.astype(np.float64)).astype(np.float32).astype(ml_dtypes.bfloat16)
    return np.stack([hi, lo], 1)


def split(x):
    hi = x.astype(BF)
    return hi, (x - hi.astype(F32)).astype(BF)


def dot(a, b):
    return jnp.dot(a, b, preferred_element_type=F32)


def left(t_ref, i, x):
    hi, lo = split(x)
    return dot(t_ref[i, 0], hi) + dot(t_ref[i, 1], hi) + dot(t_ref[i, 0], lo)


def right(x, t_ref, i):
    hi, lo = split(x)
    return dot(hi, t_ref[i, 0]) + dot(lo, t_ref[i, 0]) + dot(hi, t_ref[i, 1])


def cat(xs, axis):
    return jnp.concatenate(xs, axis)


def rows_forward(tab, wr, wi):
    e = left(tab, 0, cat([wr[:128] + wr[128:], wi[:128] + wi[128:]], 0))
    o = left(tab, 2, cat([wr[:128] - wr[128:], wi[:128] - wi[128:]], 0))
    return cat([e[:128], o[:128]], 0), cat([e[128:], o[128:]], 0)


def prepare(a, j, shift, tab, ill, amp, tiles, probe, ampo, near):
    lane = lax.broadcasted_iota(jnp.int32, (256, 128), 1)
    first = lane[:128] < 64
    ia = jnp.where(first, 2 * lane[:128], 2 * lane[:128] - 127)
    ib = jnp.where(first, 2 * lane[:128] + 1, 2 * lane[:128] - 128)
    waves = []
    for p2 in range(2):
        p = 2 * j + p2
        i = a * 4 + p
        d = shift(a, p)
        turn = lax.rem(d, 128)
        for c in range(2):
            r0 = pltpu.roll(ill[c, :, 0:128], turn, 1)
            r1 = pltpu.roll(ill[c, :, 128:256], turn, 1)
            probe[i, c] = jnp.where(lane < d, r0, r1)
            probe[i, 2 + c] = jnp.where(lane < d, r1, r0)
        pr, pi = probe[i, 0], probe[i, 1]
        tr, ti = tiles[1, a, 0], tiles[1, a, 1]
        waves.append((pr * tr - pi * ti, pr * ti + pi * tr))
        for k in (0, 1):
            x = amp[a, p, 0, pl.ds(k, 128, stride=2), :]
            y = amp[a, p, 1, pl.ds(k, 128, stride=2), :]
            if k:
                x = cat([x[64:], x[:64]], 0)
                y = cat([y[64:], y[:64]], 0)
            x = jnp.take_along_axis(x, ia, axis=1, mode="promise_in_bounds")
            y = jnp.take_along_axis(y, ib, axis=1, mode="promise_in_bounds")
            ampo[i, 0, 128 * k : 128 * k + 128] = jnp.where(first, x, y)
            ampo[i, 1, 128 * k : 128 * k + 128] = jnp.where(first, y, x)
    fr, fi = rows_forward(tab, cat([waves[0][0], waves[1][0]], 1), cat([waves[0][1], waves[1][1]], 1))
    for p2 in range(2):
        i = a * 4 + 2 * j + p2
        near[i, 0] = fr[:, 128 * p2 : 128 * p2 + 128]
        near[i, 1] = fi[:, 128 * p2 : 128 * p2 + 128]


def residual(f, amp):
    re, im = f[:, :128], f[:, 128:]
    w = 1.0 - amp * lax.rsqrt(jnp.maximum(re * re + im * im, 0.25))
    return cat([re * w, im * w], 1)


def finish(a, j, shift, tab, tiles, probe, ampo, near, acc):
    lane = lax.broadcasted_iota(jnp.int32, (256, 128), 1)
    waves, masks, backs = [], [], []
    for p2 in range(2):
        i = a * 4 + 2 * j + p2
        m = lane < shift(a, 2 * j + p2)
        masks.append(m)
        pr, pi = probe[i, 2], probe[i, 3]
        tr = jnp.where(m, tiles[2, a, 0], tiles[0, a, 0])
        ti = jnp.where(m, tiles[2, a, 1], tiles[0, a, 1])
        waves.append((pr * tr - pi * ti, pr * ti + pi * tr))
    fr, fi = rows_forward(tab, cat([waves[0][0], waves[1][0]], 1), cat([waves[0][1], waves[1][1]], 1))
    for p2 in range(2):
        i = a * 4 + 2 * j + p2
        ar, ai = near[i, 0], near[i, 1]
        br, bi = fr[:, 128 * p2 : 128 * p2 + 128], fi[:, 128 * p2 : 128 * p2 + 128]
        fe = right(cat([ar + br, ai + bi], 1), tab, 1)
        fo = right(cat([ar - br, ai - bi], 1), tab, 3)
        backs.append((right(residual(fe, ampo[i, 0]), tab, 0), right(residual(fo, ampo[i, 1]), tab, 2)))
    sums = None
    for p2 in range(2):
        i = a * 4 + 2 * j + p2
        m = masks[p2]
        be, bo = backs[p2]
        lh, rh = be + bo, be - bo
        yr = cat([lh[:, :128], rh[:, :128]], 1)
        yi = cat([lh[:, 128:], rh[:, 128:]], 1)
        e = left(tab, 1, cat([yr[:128], yi[:128]], 0))
        o = left(tab, 3, cat([yr[128:], yi[128:]], 0))
        top, bottom = e + o, e - o
        br = cat([top[:128], bottom[:128]], 0)
        bi = cat([top[128:], bottom[128:]], 0)
        pr, pi, qr, qi = probe[i, 0], probe[i, 1], probe[i, 2], probe[i, 3]
        gr = qr * br[:, 128:] + qi * bi[:, 128:]
        gi = qr * bi[:, 128:] - qi * br[:, 128:]
        parts = [
            jnp.where(m, 0.0, gr), jnp.where(m, 0.0, gi),
            pr * br[:, :128] + pi * bi[:, :128], pr * bi[:, :128] - pi * br[:, :128],
            jnp.where(m, gr, 0.0), jnp.where(m, gi, 0.0),
        ]
        sums = parts if sums is None else [x + y for x, y in zip(sums, parts)]
    for q in range(6):
        acc[a, q // 2, q % 2] += sums[q]


def kernel(
    off_hbm, t_hbm, ill_hbm, amp_hbm, proj_hbm, out_ref,
    off_ref, tab, ill, amp, tiles, probe, ampo, near, acc, send, recv,
    local_sem, pair_send, pair_recv, fwd_send, fwd_recv, all_send, all_recv, own_sem, ready,
):
    g, s = lax.axis_index("grp"), lax.axis_index("scan")
    me = g * SCAN + s
    yz, odd = s // 2, s % 2
    local = [
        pltpu.make_async_copy(proj_hbm, tiles.at[1], local_sem.at[0]),
        pltpu.make_async_copy(ill_hbm, ill, local_sem.at[1]),
        pltpu.make_async_copy(t_hbm, tab, local_sem.at[2]),
        pltpu.make_async_copy(amp_hbm.at[:, :, :, pl.ds(0, 128)], amp.at[:, :, 0], local_sem.at[3]),
        pltpu.make_async_copy(amp_hbm.at[:, :, :, pl.ds(128, 128)], amp.at[:, :, 1], local_sem.at[4]),
        pltpu.make_async_copy(off_hbm, off_ref, local_sem.at[5]),
    ]
    barrier = pltpu.get_barrier_semaphore()
    row = g * 2 + odd
    for k in range(1, 8):
        other = (row + k) % 8
        pl.semaphore_signal(
            barrier, inc=1, device_id={"grp": other // 2, "scan": yz * 2 + other % 2}, device_id_type=MESH
        )
    for k in range(1, YZ):
        pl.semaphore_signal(
            barrier, inc=1, device_id={"grp": g, "scan": (yz + k) % YZ * 2 + odd}, device_id_type=MESH
        )
    for c in local:
        c.start()
    acc[...] = jnp.zeros_like(acc)
    sends_on = jnp.logical_and(s != SCAN - 2, s != 1)
    gets = jnp.logical_and(s != 0, s != SCAN - 1)

    @pl.when(jnp.logical_not(gets))
    def _():
        tiles[2 * odd] = jnp.zeros_like(tiles[0])

    pl.semaphore_wait(barrier, 7 + YZ - 1)

    near_slot = 2 - 2 * odd
    chunks = [(a, c, h) for a in range(2) for c in range(2) for h in range(2)]

    def pair_copy(i):
        a, c, h = chunks[i]
        rows = pl.ds(128 * h, 128)
        return pltpu.make_async_remote_copy(
            proj_hbm.at[a, c, rows], tiles.at[2 * odd, a, c, rows], pair_send.at[i], pair_recv.at[i],
            device_id={"grp": g, "scan": s + 1 - 2 * odd}, device_id_type=MESH,
        )

    def fwd_copy(i):
        a, c, h = chunks[i]
        rows = pl.ds(128 * h, 128)
        return pltpu.make_async_remote_copy(
            tiles.at[near_slot, a, c, rows], tiles.at[2 * odd, a, c, rows], fwd_send.at[i], fwd_recv.at[i],
            device_id={"grp": g, "scan": s + 2 - 4 * odd}, device_id_type=MESH,
        )

    def pass_on(i):
        pair_copy(i).wait_recv()

        @pl.when(sends_on)
        def _():
            fwd_copy(i).start()

    def all_copy(a, k):
        to = (me + k) % DEVS
        return pltpu.make_async_remote_copy(
            send.at[a, to], recv.at[a, me], all_send.at[a], all_recv.at[a],
            device_id={"grp": to // SCAN, "scan": to % SCAN}, device_id_type=MESH,
        )

    def shift(a, p):
        return off_ref[a, p] - (s * 128 - 128)

    for i in range(4):
        pair_copy(i).start()
    for k in range(1, YZ):
        pl.semaphore_signal(
            ready, inc=1, device_id={"grp": g, "scan": (yz + k) % YZ * 2 + odd}, device_id_type=MESH
        )
    for c in local:
        c.wait()
    for q in range(4):
        prepare(q // 2, q % 2, shift, tab, ill, amp, tiles, probe, ampo, near)
        pass_on(q)
        pair_copy(q).wait_send()
        pair_copy(q + 4).start()

    for a in range(2):

        @pl.when(gets)
        def _():
            for i in range(4 * a, 4 * a + 4):
                fwd_copy(i).wait_recv()

        for j in range(2):
            if a == 0:
                pass_on(4 + 2 * j)
                pass_on(5 + 2 * j)
            finish(a, j, shift, tab, tiles, probe, ampo, near, acc)

        def pack(q, carry):
            for u in range(4):
                to = q * 4 + u
                for t in range(3):
                    for c in range(2):
                        send[a, to, t, 2 * c : 2 * c + 2, :] = acc[a, t, c, pl.ds(to * 2, 2), :]
            return carry

        lax.fori_loop(0, DEVS // 4, pack, 0)
        if a == 0:
            pl.semaphore_wait(ready, YZ - 1)

        def post(k, carry):
            all_copy(a, k).start()
            return carry

        lax.fori_loop(1, DEVS, post, 0)
        pltpu.make_async_copy(send.at[a, me], recv.at[a, me], own_sem.at[a]).start()

    for i in range(8):
        if i >= 4:
            pair_copy(i).wait_send()

        @pl.when(sends_on)
        def _():
            fwd_copy(i).wait_send()

    for a in range(2):
        pltpu.make_async_copy(send.at[a, me], recv.at[a, me], own_sem.at[a]).wait()
        bulk = pltpu.make_async_remote_copy(
            send.at[a, pl.ds(0, DEVS - 1)], recv.at[a, pl.ds(0, DEVS - 1)], all_send.at[a], all_recv.at[a],
            device_id={"grp": g, "scan": s + 1 - 2 * odd}, device_id_type=MESH,
        )
        bulk.wait_recv()

        def gather(h, carry):
            for t in range(SCAN):
                total = None
                for k in range(3):
                    src = t + 1 - k
                    if 0 <= src < SCAN:
                        x = recv[a, h * SCAN + src, k]
                        total = x if total is None else total + x
                for c in range(2):
                    out_ref[2 * h + a, c, :, 128 * t : 128 * t + 128] = total[2 * c : 2 * c + 2]
            return carry

        lax.fori_loop(0, GRP, gather, 0)
        bulk.wait_send()


def per_device(projection, illumination, amplitude, offsets):
    return pl.pallas_call(
        kernel,
        out_shape=jax.ShapeDtypeStruct((8, 2, 2, 4096), F32),
        in_specs=[pl.BlockSpec(memory_space=pl.ANY)] * 5,
        out_specs=pl.BlockSpec(memory_space=pltpu.VMEM),
        scratch_shapes=[
            pltpu.SMEM((2, 4), jnp.int32),
            pltpu.VMEM((4, 2, 256, 256), BF),
            pltpu.VMEM((2, 256, 256), F32),
            pltpu.VMEM((2, 4, 2, 256, 128), F32),
            pltpu.VMEM((3, 2, 2, 256, 128), F32),
            pltpu.VMEM((8, 4, 256, 128), F32),
            pltpu.VMEM((8, 2, 256, 128), F32),
            pltpu.VMEM((8, 2, 256, 128), F32),
            pltpu.VMEM((2, 3, 2, 256, 128), F32),
            pltpu.VMEM((2, DEVS, 3, 4, 128), F32),
            pltpu.VMEM((2, DEVS, 3, 4, 128), F32),
            pltpu.SemaphoreType.DMA((6,)),
            pltpu.SemaphoreType.DMA((8,)),
            pltpu.SemaphoreType.DMA((8,)),
            pltpu.SemaphoreType.DMA((8,)),
            pltpu.SemaphoreType.DMA((8,)),
            pltpu.SemaphoreType.DMA((2,)),
            pltpu.SemaphoreType.DMA((2,)),
            pltpu.SemaphoreType.DMA((2,)),
            pltpu.SemaphoreType.REGULAR,
        ],
        compiler_params=pltpu.CompilerParams(
            collective_id=0, has_side_effects=True, vmem_limit_bytes=VMEM_LIMIT
        ),
        name="gradient",
    )(offsets, jnp.asarray(tables()), illumination, amplitude, projection)


def solution(mesh):
    placed = (P("grp", None, None, "scan"), P(), P("grp", "scan", None, None), P("grp", "scan"))
    return jax.shard_map(
        per_device,
        mesh=mesh,
        in_specs=placed,
        out_specs=P(None, None, ("grp", "scan"), None),
        check_vma=False,
    )
```

time: 71.8 us -> 53.4 us (0.74)
  Pallas kernels: 64.3 us -> 51.2 us
  local copies, waits for them, and re-layouts: 5.69 us -> 1.47 us
    pallas_call x1, Pallas kernels: 64.3 us -> 51.2 us  [per_device(): pl.pallas_call(kernel, out_shape=jax.ShapeDtypeStruct((8, 2, 2, 4096), F3...]
    unnamed x9 -> x3, local copies, waits for them, and re-layouts: 5.69 us -> 1.47 us
where the time goes in v2:
time: 53.4 us; the launch traced here: 52.7 us
  Pallas kernels  51.2 us (96%)
  local copies, waits for them, and re-layouts  1.47 us (3%)
    pallas_call x1, Pallas kernels, per_device(): pl.pallas_call(kernel, out_shape=jax.ShapeDtypeStruct((8, 2, 2, 4096), F3...  51.2 us
    unnamed x3, local copies, waits for them, and re-layouts  1.47 us

profile of v2, /device:TPU:1, one launch (start us, length us, event | category | flops | bytes accessed | tf_op | source)
XLA Modules:
  0.0 52.7 jit_solution(1636898778175211515)
XLA Ops:
  0.0 0.0 copy-start
  0.0 0.7 %copy-done = s32[2,4]{1,0:T(2,128)S(1)} copy-done((s32[2,4]{1,0:T(2,128)S(1)}, s32[2,4]{1,0:T(2,128)}, u32[]{:S(2)}) %copy-start) | copy-done | bytes 56
  0.7 51.2 %gradient.1 = f32[8,2,2,4096]{3,2,1,0:T(2,128)S(1)} custom-call(s32[2,4]{1,0:T(2,128)S(1)} %copy-done, bf16[4,2,256,256]{3,2,1,0:T(8,128)(2,1)} %constant.2.clone.t_hbm, f32[2,256,256]{2,1,0:T(8,128)} %ill_hbm.1, f32[2,4,256,256]{3,2,1,0:T(8,128)} %amp_hbm.1, f32[2,2,256,128]{3,2,1,0:T(8,128)} %proj_hbm.1), custom_call_target="tpu_custom_call" | custom-call | tf_op jit(solution)/shard_map/gradient/pallas_call | solution.py:306
  51.9 0.8 %copy.7 = f32[8,2,2,4096]{3,2,1,0:T(2,128)} copy(f32[8,2,2,4096]{3,2,1,0:T(2,128)S(1)} %gradient.1) | data formatting | bytes 1048576
Async XLA Ops:
  0.0 0.7 %copy-start = (s32[2,4]{1,0:T(2,128)S(1)}, s32[2,4]{1,0:T(2,128)}, u32[]{:S(2)}) copy-start(s32[2,4]{1,0:T(2,128)} %off_hbm.1) | copy-start | bytes 100

commit v3 on v2

--- a/solution.py
+++ b/solution.py
@@ -15,6 +15,7 @@
 GRP, SCAN = 4, 32
 DEVS = GRP * SCAN
 YZ = 16
+BETWEEN = 1
 VMEM_LIMIT = 53 << 20
 
 
@@ -104,35 +105,41 @@
     return cat([re * w, im * w], 1)
 
 
-def finish(a, j, shift, tab, tiles, probe, ampo, near, acc):
+def finish(a, ps, shift, tab, tiles, probe, ampo, near, acc, between=None):
     lane = lax.broadcasted_iota(jnp.int32, (256, 128), 1)
-    waves, masks, backs = [], [], []
-    for p2 in range(2):
-        i = a * 4 + 2 * j + p2
-        m = lane < shift(a, 2 * j + p2)
-        masks.append(m)
+    index = [a * 4 + p for p in ps]
+    masks = [lane < shift(a, p) for p in ps]
+    waves = []
+    for i, m in zip(index, masks):
         pr, pi = probe[i, 2], probe[i, 3]
         tr = jnp.where(m, tiles[2, a, 0], tiles[0, a, 0])
         ti = jnp.where(m, tiles[2, a, 1], tiles[0, a, 1])
         waves.append((pr * tr - pi * ti, pr * ti + pi * tr))
-    fr, fi = rows_forward(tab, cat([waves[0][0], waves[1][0]], 1), cat([waves[0][1], waves[1][1]], 1))
-    for p2 in range(2):
-        i = a * 4 + 2 * j + p2
+    far = []
+    for q in range(0, len(ps), 2):
+        pair = waves[q : q + 2]
+        fr, fi = rows_forward(tab, cat([w[0] for w in pair], 1), cat([w[1] for w in pair], 1))
+        for u in range(len(pair)):
+            far.append((fr[:, 128 * u : 128 * u + 128], fi[:, 128 * u : 128 * u + 128]))
+    fields = []
+    for i, (br, bi) in zip(index, far):
         ar, ai = near[i, 0], near[i, 1]
-        br, bi = fr[:, 128 * p2 : 128 * p2 + 128], fi[:, 128 * p2 : 128 * p2 + 128]
-        fe = right(cat([ar + br, ai + bi], 1), tab, 1)
-        fo = right(cat([ar - br, ai - bi], 1), tab, 3)
+        fields.append((right(cat([ar + br, ai + bi], 1), tab, 1), right(cat([ar - br, ai - bi], 1), tab, 3)))
+    if between is not None:
+        between(0)
+    backs = []
+    for i, (fe, fo) in zip(index, fields):
         backs.append((right(residual(fe, ampo[i, 0]), tab, 0), right(residual(fo, ampo[i, 1]), tab, 2)))
-    sums = None
-    for p2 in range(2):
-        i = a * 4 + 2 * j + p2
-        m = masks[p2]
-        be, bo = backs[p2]
+    if between is not None:
+        between(1)
+    rows = []
+    for be, bo in backs:
         lh, rh = be + bo, be - bo
         yr = cat([lh[:, :128], rh[:, :128]], 1)
         yi = cat([lh[:, 128:], rh[:, 128:]], 1)
-        e = left(tab, 1, cat([yr[:128], yi[:128]], 0))
-        o = left(tab, 3, cat([yr[128:], yi[128:]], 0))
+        rows.append((left(tab, 1, cat([yr[:128], yi[:128]], 0)), left(tab, 3, cat([yr[128:], yi[128:]], 0))))
+    sums = None
+    for i, m, (e, o) in zip(index, masks, rows):
         top, bottom = e + o, e - o
         br = cat([top[:128], bottom[:128]], 0)
         bi = cat([top[128:], bottom[128:]], 0)
@@ -238,18 +245,26 @@
         pair_copy(q).wait_send()
         pair_copy(q + 4).start()
 
-    for a in range(2):
-
+    soon = 1 - odd
+    later = [odd, 2, 3]
+
+    def forwarded(a):
         @pl.when(gets)
         def _():
             for i in range(4 * a, 4 * a + 4):
                 fwd_copy(i).wait_recv()
 
-        for j in range(2):
-            if a == 0:
-                pass_on(4 + 2 * j)
-                pass_on(5 + 2 * j)
-            finish(a, j, shift, tab, tiles, probe, ampo, near, acc)
+    for a in range(2):
+        if a == 0:
+            pass_on(4)
+            pass_on(5)
+            pass_on(6)
+            forwarded(0)
+            finish(a, [0, 1, 2, 3], shift, tab, tiles, probe, ampo, near, acc)
+            pass_on(7)
+        else:
+            forwarded(1)
+            finish(a, [0, 1, 2, 3], shift, tab, tiles, probe, ampo, near, acc)
 
         def pack(q, carry):
             for u in range(4):

time: 53.4 us -> 46.7 us (0.87)
  Pallas kernels: 51.2 us -> 45 us
    pallas_call x1, Pallas kernels: 51.2 us -> 45 us  [per_device(): pl.pallas_call(kernel, out_shape=jax.ShapeDtypeStruct((8, 2, 2, 4096), F3...]
where the time goes in v3:
time: 46.7 us; the launch traced here: 46.5 us
  Pallas kernels  45 us (96%)
  local copies, waits for them, and re-layouts  1.47 us (3%)
    pallas_call x1, Pallas kernels, per_device(): pl.pallas_call(kernel, out_shape=jax.ShapeDtypeStruct((8, 2, 2, 4096), F3...  45 us
    unnamed x3, local copies, waits for them, and re-layouts  1.47 us

profile of v3, /device:TPU:1, one launch (start us, length us, event | category | flops | bytes accessed | tf_op | source)
XLA Modules:
  0.0 46.5 jit_solution(7667519615676830414)
XLA Ops:
  0.0 0.0 copy-start
  0.0 0.7 %copy-done = s32[2,4]{1,0:T(2,128)S(1)} copy-done((s32[2,4]{1,0:T(2,128)S(1)}, s32[2,4]{1,0:T(2,128)}, u32[]{:S(2)}) %copy-start) | copy-done | bytes 56
  0.7 45.0 %gradient.1 = f32[8,2,2,4096]{3,2,1,0:T(2,128)S(1)} custom-call(s32[2,4]{1,0:T(2,128)S(1)} %copy-done, bf16[4,2,256,256]{3,2,1,0:T(8,128)(2,1)} %constant.2.clone.t_hbm, f32[2,256,256]{2,1,0:T(8,128)} %ill_hbm.1, f32[2,4,256,256]{3,2,1,0:T(8,128)} %amp_hbm.1, f32[2,2,256,128]{3,2,1,0:T(8,128)} %proj_hbm.1), custom_call_target="tpu_custom_call" | custom-call | tf_op jit(solution)/shard_map/gradient/pallas_call | solution.py:321
  45.7 0.8 %copy.7 = f32[8,2,2,4096]{3,2,1,0:T(2,128)} copy(f32[8,2,2,4096]{3,2,1,0:T(2,128)S(1)} %gradient.1) | data formatting | bytes 1048576
Async XLA Ops:
  0.0 0.7 %copy-start = (s32[2,4]{1,0:T(2,128)S(1)}, s32[2,4]{1,0:T(2,128)}, u32[]{:S(2)}) copy-start(s32[2,4]{1,0:T(2,128)} %off_hbm.1) | copy-start | bytes 100

commit v4 on v3

--- a/solution.py
+++ b/solution.py
@@ -15,7 +15,7 @@
 GRP, SCAN = 4, 32
 DEVS = GRP * SCAN
 YZ = 16
-BETWEEN = 1
+ORDER = (3, 2, 1, 0)
 VMEM_LIMIT = 53 << 20
 
 
@@ -105,15 +105,18 @@
     return cat([re * w, im * w], 1)
 
 
-def finish(a, ps, shift, tab, tiles, probe, ampo, near, acc, between=None):
+def finish(a, ps, shift, tab, tiles, probe, ampo, near, acc, slot=None):
     lane = lax.broadcasted_iota(jnp.int32, (256, 128), 1)
     index = [a * 4 + p for p in ps]
     masks = [lane < shift(a, p) for p in ps]
     waves = []
     for i, m in zip(index, masks):
         pr, pi = probe[i, 2], probe[i, 3]
-        tr = jnp.where(m, tiles[2, a, 0], tiles[0, a, 0])
-        ti = jnp.where(m, tiles[2, a, 1], tiles[0, a, 1])
+        if slot is None:
+            tr = jnp.where(m, tiles[2, a, 0], tiles[0, a, 0])
+            ti = jnp.where(m, tiles[2, a, 1], tiles[0, a, 1])
+        else:
+            tr, ti = tiles[slot, a, 0], tiles[slot, a, 1]
         waves.append((pr * tr - pi * ti, pr * ti + pi * tr))
     far = []
     for q in range(0, len(ps), 2):
@@ -125,13 +128,9 @@
     for i, (br, bi) in zip(index, far):
         ar, ai = near[i, 0], near[i, 1]
         fields.append((right(cat([ar + br, ai + bi], 1), tab, 1), right(cat([ar - br, ai - bi], 1), tab, 3)))
-    if between is not None:
-        between(0)
     backs = []
     for i, (fe, fo) in zip(index, fields):
         backs.append((right(residual(fe, ampo[i, 0]), tab, 0), right(residual(fo, ampo[i, 1]), tab, 2)))
-    if between is not None:
-        between(1)
     rows = []
     for be, bo in backs:
         lh, rh = be + bo, be - bo
@@ -224,7 +223,7 @@
     def all_copy(a, k):
         to = (me + k) % DEVS
         return pltpu.make_async_remote_copy(
-            send.at[a, to], recv.at[a, me], all_send.at[a], all_recv.at[a],
+            send.at[a, to], recv.at[a, me], all_send.at[a], all_recv.at[a, g],
             device_id={"grp": to // SCAN, "scan": to % SCAN}, device_id_type=MESH,
         )
 
@@ -256,11 +255,12 @@
 
     for a in range(2):
         if a == 0:
+            finish(a, [soon], shift, tab, tiles, probe, ampo, near, acc, near_slot)
             pass_on(4)
             pass_on(5)
             pass_on(6)
             forwarded(0)
-            finish(a, [0, 1, 2, 3], shift, tab, tiles, probe, ampo, near, acc)
+            finish(a, later, shift, tab, tiles, probe, ampo, near, acc)
             pass_on(7)
         else:
             forwarded(1)
@@ -295,13 +295,14 @@
 
     for a in range(2):
         pltpu.make_async_copy(send.at[a, me], recv.at[a, me], own_sem.at[a]).wait()
-        bulk = pltpu.make_async_remote_copy(
-            send.at[a, pl.ds(0, DEVS - 1)], recv.at[a, pl.ds(0, DEVS - 1)], all_send.at[a], all_recv.at[a],
-            device_id={"grp": g, "scan": s + 1 - 2 * odd}, device_id_type=MESH,
-        )
-        bulk.wait_recv()
-
-        def gather(h, carry):
+
+        def bulk(n, h):
+            return pltpu.make_async_remote_copy(
+                send.at[a, pl.ds(0, n)], recv.at[a, pl.ds(0, n)], all_send.at[a], all_recv.at[a, h],
+                device_id={"grp": g, "scan": s + 1 - 2 * odd}, device_id_type=MESH,
+            )
+
+        def gather(h):
             for t in range(SCAN):
                 total = None
                 for k in range(3):
@@ -311,10 +312,12 @@
                         total = x if total is None else total + x
                 for c in range(2):
                     out_ref[2 * h + a, c, :, 128 * t : 128 * t + 128] = total[2 * c : 2 * c + 2]
-            return carry
-
-        lax.fori_loop(0, GRP, gather, 0)
-        bulk.wait_send()
+
+        for k in ORDER:
+            h = (g + k) % GRP
+            bulk(SCAN if k else SCAN - 1, h).wait_recv()
+            gather(h)
+        bulk(DEVS - 1, g).wait_send()
 
 
 def per_device(projection, illumination, amplitude, offsets):
@@ -341,7 +344,7 @@
             pltpu.SemaphoreType.DMA((8,)),
             pltpu.SemaphoreType.DMA((8,)),
             pltpu.SemaphoreType.DMA((2,)),
-            pltpu.SemaphoreType.DMA((2,)),
+            pltpu.SemaphoreType.DMA((2, GRP)),
             pltpu.SemaphoreType.DMA((2,)),
             pltpu.SemaphoreType.REGULAR,
         ],

time: 46.7 us -> 46.1 us (0.987)
  Pallas kernels: 45 us -> 44.5 us
where the time goes in v4:
time: 46.1 us; the launch traced here: 46 us
  Pallas kernels  44.5 us (97%)
  local copies, waits for them, and re-layouts  1.47 us (3%)
    pallas_call x1, Pallas kernels, per_device(): pl.pallas_call(kernel, out_shape=jax.ShapeDtypeStruct((8, 2, 2, 4096), F3...  44.5 us
    unnamed x3, local copies, waits for them, and re-layouts  1.47 us

profile of v4, /device:TPU:1, one launch (start us, length us, event | category | flops | bytes accessed | tf_op | source)
XLA Modules:
  0.0 46.0 jit_solution(4283389051032857517)
XLA Ops:
  0.0 0.0 copy-start
  0.0 0.7 %copy-done = s32[2,4]{1,0:T(2,128)S(1)} copy-done((s32[2,4]{1,0:T(2,128)S(1)}, s32[2,4]{1,0:T(2,128)}, u32[]{:S(2)}) %copy-start) | copy-done | bytes 56
  0.7 44.5 %gradient.1 = f32[8,2,2,4096]{3,2,1,0:T(2,128)S(1)} custom-call(s32[2,4]{1,0:T(2,128)S(1)} %copy-done, bf16[4,2,256,256]{3,2,1,0:T(8,128)(2,1)} %constant.2.clone.t_hbm, f32[2,256,256]{2,1,0:T(8,128)} %ill_hbm.1, f32[2,4,256,256]{3,2,1,0:T(8,128)} %amp_hbm.1, f32[2,2,256,128]{3,2,1,0:T(8,128)} %proj_hbm.1), custom_call_target="tpu_custom_call" | custom-call | tf_op jit(solution)/shard_map/gradient/pallas_call | solution.py:324
  45.2 0.8 %copy.7 = f32[8,2,2,4096]{3,2,1,0:T(2,128)} copy(f32[8,2,2,4096]{3,2,1,0:T(2,128)S(1)} %gradient.1) | data formatting | bytes 1048576
Async XLA Ops:
  0.0 0.7 %copy-start = (s32[2,4]{1,0:T(2,128)S(1)}, s32[2,4]{1,0:T(2,128)}, u32[]{:S(2)}) copy-start(s32[2,4]{1,0:T(2,128)} %off_hbm.1) | copy-start | bytes 100

commit v5 on v4

--- a/solution.py
+++ b/solution.py
@@ -15,6 +15,7 @@
 GRP, SCAN = 4, 32
 DEVS = GRP * SCAN
 YZ = 16
+BATCH = 8
 ORDER = (3, 2, 1, 0)
 VMEM_LIMIT = 53 << 20
 
@@ -263,26 +264,31 @@
             finish(a, later, shift, tab, tiles, probe, ampo, near, acc)
             pass_on(7)
         else:
+            finish(a, [soon], shift, tab, tiles, probe, ampo, near, acc, near_slot)
             forwarded(1)
-            finish(a, [0, 1, 2, 3], shift, tab, tiles, probe, ampo, near, acc)
-
-        def pack(q, carry):
-            for u in range(4):
-                to = q * 4 + u
-                for t in range(3):
-                    for c in range(2):
-                        send[a, to, t, 2 * c : 2 * c + 2, :] = acc[a, t, c, pl.ds(to * 2, 2), :]
-            return carry
-
-        lax.fori_loop(0, DEVS // 4, pack, 0)
+            finish(a, later, shift, tab, tiles, probe, ampo, near, acc)
+
+        def pack(to):
+            for t in range(3):
+                for c in range(2):
+                    send[a, to, t, 2 * c : 2 * c + 2, :] = acc[a, t, c, pl.ds(to * 2, 2), :]
+
         if a == 0:
             pl.semaphore_wait(ready, YZ - 1)
 
-        def post(k, carry):
-            all_copy(a, k).start()
+        def post(first, count):
+            for k in range(count):
+                pack((me + first + k) % DEVS)
+            for k in range(count):
+                all_copy(a, first + k).start()
+
+        def posts(q, carry):
+            post(q * BATCH + 1, BATCH)
             return carry
 
-        lax.fori_loop(1, DEVS, post, 0)
+        lax.fori_loop(0, (DEVS - 1) // BATCH, posts, 0)
+        post((DEVS - 1) // BATCH * BATCH + 1, (DEVS - 1) % BATCH)
+        pack(me)
         pltpu.make_async_copy(send.at[a, me], recv.at[a, me], own_sem.at[a]).start()
 
     for i in range(8):

time: 46.1 us -> 46.4 us (level)
  no operation moved by 1% of the time
where the time goes in v5:
time: 46.4 us; the launch traced here: 46.2 us
  Pallas kernels  44.8 us (97%)
  local copies, waits for them, and re-layouts  1.47 us (3%)
    pallas_call x1, Pallas kernels, per_device(): pl.pallas_call(kernel, out_shape=jax.ShapeDtypeStruct((8, 2, 2, 4096), F3...  44.8 us
    unnamed x3, local copies, waits for them, and re-layouts  1.47 us

profile of v5, /device:TPU:1, one launch (start us, length us, event | category | flops | bytes accessed | tf_op | source)
XLA Modules:
  0.0 46.2 jit_solution(3946693753968752359)
XLA Ops:
  0.0 0.0 copy-start
  0.0 0.7 %copy-done = s32[2,4]{1,0:T(2,128)S(1)} copy-done((s32[2,4]{1,0:T(2,128)S(1)}, s32[2,4]{1,0:T(2,128)}, u32[]{:S(2)}) %copy-start) | copy-done | bytes 56
  0.7 44.8 %gradient.1 = f32[8,2,2,4096]{3,2,1,0:T(2,128)S(1)} custom-call(s32[2,4]{1,0:T(2,128)S(1)} %copy-done, bf16[4,2,256,256]{3,2,1,0:T(8,128)(2,1)} %constant.2.clone.t_hbm, f32[2,256,256]{2,1,0:T(8,128)} %ill_hbm.1, f32[2,4,256,256]{3,2,1,0:T(8,128)} %amp_hbm.1, f32[2,2,256,128]{3,2,1,0:T(8,128)} %proj_hbm.1), custom_call_target="tpu_custom_call" | custom-call | tf_op jit(solution)/shard_map/gradient/pallas_call | solution.py:330
  45.4 0.8 %copy.7 = f32[8,2,2,4096]{3,2,1,0:T(2,128)} copy(f32[8,2,2,4096]{3,2,1,0:T(2,128)S(1)} %gradient.1) | data formatting | bytes 1048576
Async XLA Ops:
  0.0 0.7 %copy-start = (s32[2,4]{1,0:T(2,128)S(1)}, s32[2,4]{1,0:T(2,128)}, u32[]{:S(2)}) copy-start(s32[2,4]{1,0:T(2,128)} %off_hbm.1) | copy-start | bytes 100
